TPU v7x, 256 devices: a whole 4x4x8 slice. The times are simulated.
256 devices in a mesh: dp: 8 (over z_lo, core), expert: 32 (over z_hi, y, x).
Axes of the slice: x: 4, y: 4, z: 8 (z_hi: 2, z_lo: 4; z = z_hi * 4 + z_lo), core: 2. Of those that a mesh axis runs over, the one named last changes fastest.
Arguments:
- tokens: bfloat16 [65536, 1280], P(('dp', 'expert')), may hold values from -24 to 24
- router: bfloat16 [1280, 64], replicated, may hold values from -11 to 11
- w_in: bfloat16 [64, 1280, 4096], P('expert', None, 'dp'), may hold values from -0.15625 to 0.15625
- w_out: bfloat16 [64, 4096, 1280], P('expert', 'dp'), may hold values from -0.09375 to 0.09375
- out_grad: bfloat16 [65536, 1280], P(('dp', 'expert')), may hold values from -6 to 6
Outputs:
- token_grad: bfloat16 [65536, 1280], P(('dp', 'expert'))
- router_grad: float32 [1280, 64], replicated
- w_in_grad: bfloat16 [64, 1280, 4096], P('expert', None, 'dp')
- w_out_grad: bfloat16 [64, 4096, 1280], P('expert', 'dp')
All inputs are finite; a program needn't handle non-finite values.
Results may differ from a plain program's by a relative error of at most 0.012.
Values may be sent and summed in bfloat16 or wider, within the bound.
A program may use at most 64 MiB of HBM per device.

v0:
```python
import jax
import jax.numpy as jnp
from jax import lax
from jax.sharding import Mesh
from jax.sharding import PartitionSpec as P

M = 256
DP = ("dp_0", "dp_1")
DP_EXPERT = ("dp_0", "dp_1", "expert")


def laid_out(blocks, dim):
    blocks = jnp.moveaxis(blocks, 0, dim)
    lengths = blocks.shape
    return blocks.reshape(*lengths[:dim], lengths[dim] * lengths[dim + 1], *lengths[dim + 2 :])


def gather_in_order(value, axes, order):
    blocks = value
    for k in order:
        blocks = lax.all_gather(blocks, axes[k])
    done = order[::-1]
    back = [done.index(k) for k in range(len(axes))]
    blocks = blocks.transpose(*back, *range(len(axes), blocks.ndim))
    return blocks.reshape(-1, *value.shape)


def gathered_by_axis(value, axes, order, dim):
    return laid_out(gather_in_order(value, axes, order), dim)


def activate(values):
    return jax.nn.gelu(values, approximate=True)


def to_experts(slot_rows):
    placed = lax.all_to_all(slot_rows, "expert", split_axis=1, concat_axis=0, tiled=True)
    return gathered_by_axis(placed, DP, (0, 1), 0)


def to_owners(partial_value):
    summed = lax.psum_scatter(partial_value, DP, scatter_dimension=0, tiled=True).astype(
        jnp.bfloat16
    )
    return lax.all_to_all(summed, "expert", split_axis=0, concat_axis=1, tiled=True)


def local(tokens, router, w_in, w_out, out_grad):
    images = tokens.shape[0] // M
    feature = tokens.shape[1]
    inputs = tokens.reshape(images, M, feature)
    grads = out_grad.reshape(images, M, feature)
    logits = jnp.einsum("bmd,de->bme", inputs, router, preferred_element_type=jnp.float32)
    dispatch = jax.nn.softmax(logits, axis=1)
    combine = jax.nn.softmax(logits, axis=2)
    dispatch_b = dispatch.astype(jnp.bfloat16)
    combine_b = combine.astype(jnp.bfloat16)
    slots = jnp.einsum(
        "bme,bmd->bed", dispatch_b, inputs, preferred_element_type=jnp.float32
    ).astype(jnp.bfloat16)
    slot_rows = to_experts(slots)
    hidden = jnp.einsum("red,edf->ref", slot_rows, w_in, preferred_element_type=jnp.float32)
    active, pull = jax.vjp(activate, hidden)
    active_b = active.astype(jnp.bfloat16)
    partial_value = jnp.einsum("ref,efd->red", active_b, w_out, preferred_element_type=jnp.float32)
    slot_out = to_owners(partial_value)
    slot_grad = jnp.einsum(
        "bme,bmd->bed", combine_b, grads, preferred_element_type=jnp.float32
    ).astype(jnp.bfloat16)
    grad_rows = to_experts(slot_grad)
    active_grad = jnp.einsum("red,efd->ref", grad_rows, w_out, preferred_element_type=jnp.float32)
    second_grad = jnp.einsum(
        "ref,red->efd", active_b, grad_rows, preferred_element_type=jnp.float32
    ).astype(jnp.bfloat16)
    hidden_grad = pull(active_grad)[0].astype(jnp.bfloat16)
    first_grad = jnp.einsum(
        "red,ref->edf", slot_rows, hidden_grad, preferred_element_type=jnp.float32
    ).astype(jnp.bfloat16)
    input_partial = jnp.einsum(
        "ref,edf->red", hidden_grad, w_in, preferred_element_type=jnp.float32
    )
    slot_in_grad = to_owners(input_partial)
    combine_grad = jnp.einsum("bmd,bed->bme", grads, slot_out, preferred_element_type=jnp.float32)
    dispatch_grad = jnp.einsum(
        "bmd,bed->bme", inputs, slot_in_grad, preferred_element_type=jnp.float32
    )
    logit_grad = combine * (combine_grad - jnp.sum(combine_grad * combine, axis=2, keepdims=True))
    logit_grad = logit_grad + dispatch * (
        dispatch_grad - jnp.sum(dispatch_grad * dispatch, axis=1, keepdims=True)
    )
    logit_b = logit_grad.astype(jnp.bfloat16)
    token_grad = jnp.einsum(
        "bme,bed->bmd", dispatch_b, slot_in_grad, preferred_element_type=jnp.float32
    )
    token_grad = token_grad + jnp.einsum(
        "bme,de->bmd", logit_b, router, preferred_element_type=jnp.float32
    )
    router_part = jnp.einsum("bmd,bme->de", inputs, logit_b, preferred_element_type=jnp.float32)
    router_grad = lax.psum(router_part, DP_EXPERT)
    return (
        token_grad.astype(jnp.bfloat16).reshape(images * M, feature),
        router_grad,
        first_grad,
        second_grad,
    )


def solution(mesh):
    split = Mesh(mesh.devices.reshape(4, 2, mesh.shape["expert"]), ("dp_0", "dp_1", "expert"))
    placed = (
        P(DP_EXPERT, None),
        P(),
        P("expert", None, DP),
        P("expert", DP, None),
        P(DP_EXPERT, None),
    )
    return jax.shard_map(
        local,
        mesh=split,
        in_specs=placed,
        out_specs=(P(DP_EXPERT, None), P(), P("expert", None, DP), P("expert", DP, None)),
        check_vma=False,
    )
```

profile of v0, /device:TPU:1, one launch (start us, length us, event | category | flops | bytes accessed | tf_op | source)
XLA Modules:
  0.0 484.6 jit_solution(391703074439383236)
XLA Ops:
  7.2 1.7 fusion.21
  9.0 0.2 fusion.13
  9.2 1.4 fusion.2
  10.5 0.3 copy.45
  10.8 0.5 broadcast.53
  11.3 1.6 reduce.16
  13.0 25.8 %all_to_all.42 = bf16[32,2,1280]{2,1,0:T(2,128)(2,1)S(1)} all-to-all(bf16[32,2,1280]{2,1,0:T(2,128)(2,1)S(1)} %reshape.119), channel_id=1, replica_groups=mesh['dp_0'=4,'dp_1'=2,'expert'=32] {'expert'}, dimensions={0} | all-to-all | bytes 327680 | tf_op jit(solution)/shard_map/all_to_all | solution.py:37
  38.8 0.1 reshape.120
  38.9 0.9 bitcast_reduce_fusion.1
  39.9 15.2 %all_gather.23 = bf16[4,32,2,1280]{3,1,2,0:T(8,128)(2,1)} all-gather(bf16[1,32,2,1280]{3,1,2,0:T(8,128)(2,1)S(1)} %copy.33), channel_id=1, replica_groups=mesh['dp_0'=4,'dp_1'=2,'expert'=32] {'dp_0'}, dimensions={0}, use_global_device_ids=true | all-gather | bytes 819200 | tf_op jit(solution)/shard_map/all_gather | solution.py:21
  55.3 1.3 fusion.1
  56.6 0.3 copy.46
  56.8 1.6 reduce.17
  58.5 15.0 %all_to_all.43 = bf16[32,2,1280]{2,1,0:T(2,128)(2,1)S(1)} all-to-all(bf16[32,2,1280]{2,1,0:T(2,128)(2,1)S(1)} %reshape.121), channel_id=1, replica_groups=mesh['dp_0'=4,'dp_1'=2,'expert'=32] {'expert'}, dimensions={0} | all-to-all | bytes 327680 | tf_op jit(solution)/shard_map/all_to_all | solution.py:37
  73.5 0.1 reshape.122
  73.6 0.9 bitcast_reduce_fusion
  74.6 14.8 %all_gather.20 = bf16[4,32,2,1280]{3,1,2,0:T(8,128)(2,1)} all-gather(bf16[1,32,2,1280]{3,1,2,0:T(8,128)(2,1)S(1)} %copy.30), channel_id=1, replica_groups=mesh['dp_0'=4,'dp_1'=2,'expert'=32] {'dp_0'}, dimensions={0}, use_global_device_ids=true | all-gather | bytes 819200 | tf_op jit(solution)/shard_map/all_gather | solution.py:21
  89.5 2.5 copy.34
  92.0 15.6 %all-gather.5.cloned.1.call-done = bf16[8,32,2,1280]{3,1,2,0:T(8,128)(2,1)} async-done(((bf16[4,32,2,1280]{3,1,2,0:T(8,128)(2,1)}), bf16[8,32,2,1280]{3,1,2,0:T(8,128)(2,1)}) %all-gather.5.cloned.1.call-update) | async-done | bytes 1310736 | tf_op jit(solution)/shard_map/all_gather | solution.py:21
  107.6 1.5 copy.31
  109.1 0.2 copy-done.1
  109.3 0.8 convolution_bitcast_fusion.3
  110.1 1.6 copy-done.5
  111.7 1.3 fusion.9
  113.1 0.8 copy-done.6
  113.8 2.4 convolution_bitcast_fusion.1
  116.3 4.5 convolution_bitcast_fusion
  120.8 4.1 convolution_convert_fusion
  124.9 32.3 %reduce-scatter.3.cloned.1.call-done = f32[32,2,1280]{2,0,1:T(8,128)} async-done(((f32[256,2,1280]{2,0,1:T(8,128)}), f32[32,2,1280]{2,0,1:T(8,128)}) %reduce-scatter.3.cloned.1.call-update) | async-done | bytes 327696 | tf_op jit(solution)/shard_map/reduce_scatter | solution.py:42
  157.2 1.0 convert_element_type.53
  158.2 0.8 copy.35
  159.0 11.1 %all-to-all-start.2 = ((bf16[32,2,1280]{2,1,0:T(2,128)(2,1)}), bf16[32,2,1280]{2,1,0:T(2,128)(2,1)S(1)}, u32[]{:S(2)}, u32[]{:S(2)}) async-start(bf16[32,2,1280]{2,1,0:T(2,128)(2,1)} %copy.35), calls=%async_computation.3 | async-start | bytes 327680 | tf_op jit(solution)/shard_map/all_to_all | solution.py:45
  170.1 3.9 convolution_convert_fusion.1
  174.0 29.4 %reduce-scatter.5.cloned.1.call-done = f32[32,2,1280]{2,0,1:T(8,128)} async-done(((f32[256,2,1280]{2,0,1:T(8,128)}), f32[32,2,1280]{2,0,1:T(8,128)}) %reduce-scatter.5.cloned.1.call-update) | async-done | bytes 327696 | tf_op jit(solution)/shard_map/reduce_scatter | solution.py:42
  203.4 1.0 convert_element_type.55
  204.4 0.8 copy.36
  205.3 10.4 %all-to-all-start.3 = ((bf16[32,2,1280]{2,1,0:T(2,128)(2,1)}), bf16[32,2,1280]{2,1,0:T(2,128)(2,1)}, u32[]{:S(2)}, u32[]{:S(2)}) async-start(bf16[32,2,1280]{2,1,0:T(2,128)(2,1)} %copy.36), calls=%async_computation.5 | async-start | bytes 327680 | tf_op jit(solution)/shard_map/all_to_all | solution.py:45
  215.7 1.0 reshape.113
  216.7 1.0 convolution_bitcast_fusion.5
  217.6 1.5 fusion.15
  219.1 7.9 %all-to-all-done.3 = bf16[32,2,1280]{2,1,0:T(2,128)(2,1)} async-done(((bf16[32,2,1280]{2,1,0:T(2,128)(2,1)}), bf16[32,2,1280]{2,1,0:T(2,128)(2,1)}, u32[]{:S(2)}, u32[]{:S(2)}) %all-to-all-start.3) | async-done | bytes 163872 | tf_op jit(solution)/shard_map/all_to_all | solution.py:45
  227.0 1.6 reshape.114
  228.7 1.6 multiply_reduce_fusion.1
  230.3 0.6 copy-done.9
  230.9 1.9 convolution_bitcast_fusion.2
  232.8 2.7 fusion
  235.4 240.9 %all-reduce.2.cloned.1.call-done = f32[1280,64]{0,1:T(8,128)} async-done(((f32[1280,64]{0,1:T(8,128)}), f32[1280,64]{0,1:T(8,128)}) %all-reduce.2.cloned.1.call-update) | async-done | bytes 327696 | tf_op jit(solution)/shard_map/psum | solution.py:99
  476.3 1.7 copy.50
  (34 shorter events, 0.7 us)
Async XLA Ops:
  7.2 101.9 %copy-start = (bf16[2,1280,512]{2,1,0:T(8,128)(2,1)S(1)}, bf16[2,1280,512]{2,1,0:T(8,128)(2,1)}, u32[]{:S(2)}) copy-start(bf16[2,1280,512]{2,1,0:T(8,128)(2,1)} %param.7) | copy-start | bytes 7864324
  7.2 82.3 %all-gather.7.cloned.1.call-start = ((), (), s32[]{:S(2)}) async-start(), calls=%async_computation.10 | async-start | bytes 1966080 | tf_op jit(solution)/shard_map/all_gather | solution.py:21
  55.2 52.3 %all-gather.5.cloned.1.call-start = ((), (), s32[]{:S(2)}) async-start(), calls=%async_computation.9 | async-start | bytes 1966080 | tf_op jit(solution)/shard_map/all_gather | solution.py:21
  89.4 67.8 %reduce-scatter.3.cloned.1.call-start = ((), (), s32[]{:S(2)}) async-start(), calls=%async_computation.6 | async-start | bytes 2949120 | tf_op jit(solution)/shard_map/reduce_scatter | solution.py:42
  107.6 1.7 copy-start.1
  109.1 4.0 copy-start.4
  109.1 2.6 copy-start.5
  110.1 2.9 copy-start.3
  113.0 0.8 copy-start.6
  116.3 87.1 %reduce-scatter.5.cloned.1.call-start = ((), (), s32[]{:S(2)}) async-start(), calls=%async_computation.7 | async-start | bytes 2949120 | tf_op jit(solution)/shard_map/reduce_scatter | solution.py:42
  159.0 46.3 %all-to-all-start.2 = ((bf16[32,2,1280]{2,1,0:T(2,128)(2,1)}), bf16[32,2,1280]{2,1,0:T(2,128)(2,1)S(1)}, u32[]{:S(2)}, u32[]{:S(2)}) async-start(bf16[32,2,1280]{2,1,0:T(2,128)(2,1)} %copy.35), calls=%async_computation.3 | async-start | bytes 327680 | tf_op jit(solution)/shard_map/all_to_all | solution.py:45
  170.1 46.5 %copy-start.2 = (bf16[256,1280]{1,0:T(8,128)(2,1)S(1)}, bf16[256,1280]{1,0:T(8,128)(2,1)}, u32[]{:S(2)}) copy-start(bf16[256,1280]{1,0:T(8,128)(2,1)} %param.5) | copy-start | bytes 1966084
  205.3 10.4 %copy-start.8 = (bf16[32,2,1280]{2,1,0:T(2,128)(2,1)}, bf16[32,2,1280]{2,1,0:T(2,128)(2,1)S(1)}, u32[]{:S(2)}) copy-start(bf16[32,2,1280]{2,1,0:T(2,128)(2,1)S(1)} %all-to-all-done.2) | copy-start | bytes 491524
  205.3 21.8 %all-to-all-start.3 = ((bf16[32,2,1280]{2,1,0:T(2,128)(2,1)}), bf16[32,2,1280]{2,1,0:T(2,128)(2,1)}, u32[]{:S(2)}, u32[]{:S(2)}) async-start(bf16[32,2,1280]{2,1,0:T(2,128)(2,1)} %copy.36), calls=%async_computation.5 | async-start | bytes 327680 | tf_op jit(solution)/shard_map/all_to_all | solution.py:45
  215.6 260.7 %all-reduce.2.cloned.1.call-start = ((), (), s32[]{:S(2)}) async-start(), calls=%async_computation.8 | async-start | bytes 655360 | tf_op jit(solution)/shard_map/psum | solution.py:99
  219.1 13.6 %copy-start.7 = (bf16[1280,64]{0,1:T(8,128)(2,1)S(1)}, bf16[1280,64]{0,1:T(8,128)(2,1)}, u32[]{:S(2)}) copy-start(bf16[1280,64]{0,1:T(8,128)(2,1)} %param.6) | copy-start | bytes 491524
  230.3 0.6 copy-start.9
Sparse Core Ops, SparseCore 0:
  55.3 13.8 all-gather.6
  89.5 17.9 all-gather.4
  116.4 40.7 reduce-scatter.2
  159.6 43.8 reduce-scatter.4
  232.9 243.3 all-reduce.1
where the time goes:
time: 485 us
  waiting for transfers between devices  326 us (67%)
  blocking collectives  70.8 us (15%)
  matrix products  30 us (6%)
  starting transfers between devices  21.7 us (4%)
  local copies, waits for them, and re-layouts  16.6 us (3%)
  between operations  14 us (3%)
  other arithmetic  5.36 us (1%)
    psum x1, waiting for transfers between devices, local(): router_grad = lax.psum(router_part, DP_EXPERT)  241 us
    reduce_scatter x2, waiting for transfers between devices, to_owners(): lax.psum_scatter(partial_value, DP, scatter_dimension=0, tiled=True)  61.7 us
    all_to_all x2, blocking collectives, to_experts(): lax.all_to_all(slot_rows, 'expert', split_axis=1, concat_axis=0, tiled=True)  40.8 us
    all_gather x2, blocking collectives, gather_in_order(): blocks = lax.all_gather(blocks, axes[k])  30 us
    all_to_all x2, starting transfers between devices, to_owners(): lax.all_to_all(summed, 'expert', split_axis=0, concat_axis=1, tiled=True)  21.5 us
    all_gather x2, waiting for transfers between devices, gather_in_order(): blocks = lax.all_gather(blocks, axes[k])  15.6 us
  transfers between devices with their start and end apart: 7, of which 5 were waited for; matrix products, arithmetic and copies ran while one was open for 6% of the time, Pallas kernels for 0%

commit v1 on v0

--- a/solution.py
+++ b/solution.py
@@ -96,7 +96,7 @@
         "bme,de->bmd", logit_b, router, preferred_element_type=jnp.float32
     )
     router_part = jnp.einsum("bmd,bme->de", inputs, logit_b, preferred_element_type=jnp.float32)
-    router_grad = lax.psum(router_part, DP_EXPERT)
+    router_grad = lax.psum(lax.psum(router_part, axis_name="dp_0"), axis_name=("dp_1", "expert"))
     return (
         token_grad.astype(jnp.bfloat16).reshape(images * M, feature),
         router_grad,

time: 485 us -> 1090 us (2.25); the launches traced: 485 us -> 1070 us
  waiting for transfers between devices: 326 us -> 916 us
    psum x1 -> x2, waiting for transfers between devices: 241 us -> 825 us  [the longest x1 783 us: local(): lax.psum(lax.psum(router_part, axis_name='dp_0'), axis_name=('dp_1', 'exp...]
  transfers between devices with their start and end apart: 7 -> 8, of which waited for: 5 -> 6; matrix products, arithmetic and copies ran while one was open for 6% -> 2% of each run, Pallas kernels for 0% -> 0%
where the time goes in v1:
time: 1090 us; the launch traced here: 1070 us
  waiting for transfers between devices  916 us (84%)
  blocking collectives  70.8 us (6%)
  matrix products  27.5 us (3%)
  starting transfers between devices  21.8 us (2%)
  local copies, waits for them, and re-layouts  17.2 us (2%)
  between operations  14.4 us (1%)
    psum x1, waiting for transfers between devices, local(): lax.psum(lax.psum(router_part, axis_name='dp_0'), axis_name=('dp_1', 'exp...  783 us
    reduce_scatter x2, waiting for transfers between devices, to_owners(): lax.psum_scatter(partial_value, DP, scatter_dimension=0, tiled=True)  70.2 us
    psum x1, waiting for transfers between devices, local(): lax.psum(router_part, axis_name='dp_0')  42.3 us
    all_to_all x2, blocking collectives, to_experts(): lax.all_to_all(slot_rows, 'expert', split_axis=1, concat_axis=0, tiled=True)  40.8 us
    all_gather x2, blocking collectives, gather_in_order(): blocks = lax.all_gather(blocks, axes[k])  30 us
  transfers between devices with their start and end apart: 8, of which 6 were waited for; matrix products, arithmetic and copies ran while one was open for 2% of the time, Pallas kernels for 0%

profile of v1, /device:TPU:1, one launch (start us, length us, event | category | flops | bytes accessed | tf_op | source)
XLA Modules:
  0.0 1073.2 jit_solution(10684066237586223130)
XLA Ops:
  7.2 1.7 fusion.21
  9.0 0.2 fusion.13
  9.2 1.4 fusion.2
  10.5 0.3 copy.45
  10.8 0.5 broadcast.53
  11.3 1.6 reduce.16
  13.0 25.8 %all_to_all.42 = bf16[32,2,1280]{2,1,0:T(2,128)(2,1)S(1)} all-to-all(bf16[32,2,1280]{2,1,0:T(2,128)(2,1)S(1)} %reshape.119), channel_id=1, replica_groups=mesh['dp_0'=4,'dp_1'=2,'expert'=32] {'expert'}, dimensions={0} | all-to-all | bytes 327680 | tf_op jit(solution)/shard_map/all_to_all | solution.py:37
  38.9 0.9 bitcast_reduce_fusion.1
  39.9 15.2 %all_gather.23 = bf16[4,32,2,1280]{3,1,2,0:T(8,128)(2,1)} all-gather(bf16[1,32,2,1280]{3,1,2,0:T(8,128)(2,1)S(1)} %copy.33), channel_id=1, replica_groups=mesh['dp_0'=4,'dp_1'=2,'expert'=32] {'dp_0'}, dimensions={0}, use_global_device_ids=true | all-gather | bytes 819200 | tf_op jit(solution)/shard_map/all_gather | solution.py:21
  55.3 1.3 fusion.1
  56.6 0.3 copy.46
  56.8 1.6 reduce.17
  58.5 15.0 %all_to_all.43 = bf16[32,2,1280]{2,1,0:T(2,128)(2,1)S(1)} all-to-all(bf16[32,2,1280]{2,1,0:T(2,128)(2,1)S(1)} %reshape.121), channel_id=1, replica_groups=mesh['dp_0'=4,'dp_1'=2,'expert'=32] {'expert'}, dimensions={0} | all-to-all | bytes 327680 | tf_op jit(solution)/shard_map/all_to_all | solution.py:37
  73.6 0.9 bitcast_reduce_fusion
  74.6 14.8 %all_gather.20 = bf16[4,32,2,1280]{3,1,2,0:T(8,128)(2,1)} all-gather(bf16[1,32,2,1280]{3,1,2,0:T(8,128)(2,1)S(1)} %copy.30), channel_id=1, replica_groups=mesh['dp_0'=4,'dp_1'=2,'expert'=32] {'dp_0'}, dimensions={0}, use_global_device_ids=true | all-gather | bytes 819200 | tf_op jit(solution)/shard_map/all_gather | solution.py:21
  89.5 2.5 copy.34
  92.0 15.6 %all-gather.5.cloned.1.call-done = bf16[8,32,2,1280]{3,1,2,0:T(8,128)(2,1)} async-done(((bf16[4,32,2,1280]{3,1,2,0:T(8,128)(2,1)}), bf16[8,32,2,1280]{3,1,2,0:T(8,128)(2,1)}) %all-gather.5.cloned.1.call-update) | async-done | bytes 1310736 | tf_op jit(solution)/shard_map/all_gather | solution.py:21
  107.6 1.5 copy.31
  109.3 0.8 convolution_bitcast_fusion.3
  110.1 1.6 copy-done.5
  111.7 1.3 fusion.9
  113.1 0.8 copy-done.6
  113.8 2.4 convolution_bitcast_fusion.1
  116.3 4.4 convolution_bitcast_fusion
  120.8 36.4 %reduce-scatter.3.cloned.1.call-done = f32[32,2,1280]{2,0,1:T(8,128)} async-done(((f32[256,2,1280]{2,0,1:T(8,128)}), f32[32,2,1280]{2,0,1:T(8,128)}) %reduce-scatter.3.cloned.1.call-update) | async-done | bytes 327696 | tf_op jit(solution)/shard_map/reduce_scatter | solution.py:42
  157.2 1.0 convert_element_type.53
  158.2 0.8 copy.35
  159.0 10.9 %all-to-all-start.2 = ((bf16[32,2,1280]{2,1,0:T(2,128)(2,1)}), bf16[32,2,1280]{2,1,0:T(2,128)(2,1)S(1)}, u32[]{:S(2)}, u32[]{:S(2)}) async-start(bf16[32,2,1280]{2,1,0:T(2,128)(2,1)} %copy.35), calls=%async_computation.3 | async-start | bytes 327680 | tf_op jit(solution)/shard_map/all_to_all | solution.py:45
  169.9 33.9 %reduce-scatter.5.cloned.1.call-done = f32[32,2,1280]{2,0,1:T(8,128)} async-done(((f32[256,2,1280]{2,0,1:T(8,128)}), f32[32,2,1280]{2,0,1:T(8,128)}) %reduce-scatter.5.cloned.1.call-update) | async-done | bytes 327696 | tf_op jit(solution)/shard_map/reduce_scatter | solution.py:42
  203.8 1.0 convert_element_type.55
  204.8 0.8 copy.36
  205.6 0.7 copy-done.8
  206.3 10.4 all-to-all-start.3
  216.7 0.2 all-reduce.3.cloned.1.call-start
  217.0 4.1 convolution_convert_fusion
  221.0 1.0 reshape.113
  222.0 1.0 convolution_bitcast_fusion.5
  223.0 5.1 all-to-all-done.3
  228.1 1.6 reshape.114
  229.8 1.6 multiply_reduce_fusion.1
  231.4 0.6 copy-done.10
  232.0 1.9 convolution_bitcast_fusion.2
  233.9 3.9 convolution_convert_fusion.1
  237.8 42.3 %all-reduce.3.cloned.1.call-done = f32[1280,64]{0,1:T(8,128)} async-done(((f32[1280,64]{0,1:T(8,128)}), f32[1280,64]{0,1:T(8,128)}) %all-reduce.3.cloned.1.call-update) | async-done | bytes 327696 | tf_op jit(solution)/shard_map/psum | solution.py:99
  280.2 0.4 fusion.15
  280.6 1.3 fusion
  281.9 782.7 %all-reduce.5.cloned.1.call-done = f32[1280,64]{0,1:T(8,128)} async-done(((f32[1280,64]{0,1:T(8,128)}), f32[1280,64]{0,1:T(8,128)}) %all-reduce.5.cloned.1.call-update) | async-done | bytes 327696 | tf_op jit(solution)/shard_map/psum | solution.py:99
  1064.6 1.7 copy.51
  (41 shorter events, 1.1 us)
Async XLA Ops:
  7.2 101.9 %copy-start = (bf16[2,1280,512]{2,1,0:T(8,128)(2,1)S(1)}, bf16[2,1280,512]{2,1,0:T(8,128)(2,1)}, u32[]{:S(2)}) copy-start(bf16[2,1280,512]{2,1,0:T(8,128)(2,1)} %param.7) | copy-start | bytes 7864324
  7.2 82.3 %all-gather.7.cloned.1.call-start = ((), (), s32[]{:S(2)}) async-start(), calls=%async_computation.11 | async-start | bytes 1966080 | tf_op jit(solution)/shard_map/all_gather | solution.py:21
  55.2 52.3 %all-gather.5.cloned.1.call-start = ((), (), s32[]{:S(2)}) async-start(), calls=%async_computation.10 | async-start | bytes 1966080 | tf_op jit(solution)/shard_map/all_gather | solution.py:21
  89.4 67.8 %reduce-scatter.3.cloned.1.call-start = ((), (), s32[]{:S(2)}) async-start(), calls=%async_computation.6 | async-start | bytes 2949120 | tf_op jit(solution)/shard_map/reduce_scatter | solution.py:42
  107.6 1.7 copy-start.1
  109.1 4.0 copy-start.4
  109.1 2.6 copy-start.5
  110.1 2.9 copy-start.3
  113.0 0.8 copy-start.6
  116.3 87.5 %reduce-scatter.5.cloned.1.call-start = ((), (), s32[]{:S(2)}) async-start(), calls=%async_computation.7 | async-start | bytes 2949120 | tf_op jit(solution)/shard_map/reduce_scatter | solution.py:42
  159.0 46.6 %all-to-all-start.2 = ((bf16[32,2,1280]{2,1,0:T(2,128)(2,1)}), bf16[32,2,1280]{2,1,0:T(2,128)(2,1)S(1)}, u32[]{:S(2)}, u32[]{:S(2)}) async-start(bf16[32,2,1280]{2,1,0:T(2,128)(2,1)} %copy.35), calls=%async_computation.3 | async-start | bytes 327680 | tf_op jit(solution)/shard_map/all_to_all | solution.py:45
  205.6 0.7 copy-start.8
  206.3 21.8 %all-to-all-start.3 = ((bf16[32,2,1280]{2,1,0:T(2,128)(2,1)}), bf16[32,2,1280]{2,1,0:T(2,128)(2,1)}, u32[]{:S(2)}, u32[]{:S(2)}) async-start(bf16[32,2,1280]{2,1,0:T(2,128)(2,1)} %copy.36), calls=%async_computation.5 | async-start | bytes 327680 | tf_op jit(solution)/shard_map/all_to_all | solution.py:45
  216.7 5.3 copy-start.2
  216.7 63.4 %all-reduce.3.cloned.1.call-start = ((), (), s32[]{:S(2)}) async-start(), calls=%async_computation.8 | async-start | bytes 655360 | tf_op jit(solution)/shard_map/psum | solution.py:99
  231.4 0.6 copy-start.10
  233.9 46.8 %copy-start.7 = (bf16[1280,64]{0,1:T(8,128)(2,1)S(1)}, bf16[1280,64]{0,1:T(8,128)(2,1)}, u32[]{:S(2)}) copy-start(bf16[1280,64]{0,1:T(8,128)(2,1)} %param.6) | copy-start | bytes 491524
  233.9 46.8 %copy-start.9 = (f32[256,64]{0,1:T(8,128)S(1)}, f32[256,64]{0,1:T(8,128)}, u32[]{:S(2)}) copy-start(f32[256,64]{0,1:T(8,128)} %convolution_bitcast_fusion.5) | copy-start | bytes 196612
  233.9 46.8 %copy-start.11 = (f32[256,64]{0,1:T(8,128)S(1)}, f32[256,64]{0,1:T(8,128)}, u32[]{:S(2)}) copy-start(f32[256,64]{0,1:T(8,128)} %copy-done.10) | copy-start | bytes 196612
  233.9 830.7 %all-reduce.5.cloned.1.call-start = ((), (), s32[]{:S(2)}) async-start(), calls=%async_computation.9 | async-start | bytes 655360 | tf_op jit(solution)/shard_map/psum | solution.py:99
Sparse Core Ops, SparseCore 0:
  55.3 13.8 all-gather.6
  89.5 17.9 all-gather.4
  116.4 40.7 reduce-scatter.2
  160.1 43.6 reduce-scatter.4
  234.0 46.1 all-reduce.2
  282.6 781.9 all-reduce.4
